TPU v7x, 128 devices: a whole 4x4x4 slice. The times are simulated.
128 devices in a mesh: member: 8 (over z, y_hi), mp: 16 (over x, y_lo, core).
Axes of the slice: x: 4, y: 4 (y_hi: 2, y_lo: 2; y = y_hi * 2 + y_lo), z: 4, core: 2. Of those that a mesh axis runs over, the one named last changes fastest.
Arguments:
- grid_point_features: bfloat16 [8, 8192, 1024], P('member', 'mp'), may hold values from -6 to 6
- projection_weights_qkv: bfloat16 [1024, 3072], replicated, may hold values from -0.75 to 0.75
- merging_projection: bfloat16 [1024, 1024], replicated, may hold values from -0.1875 to 0.1875
- readout_weights_table: bfloat16 [1024, 128], replicated, may hold values from -0.1875 to 0.1875
- observed: float32 [8192, 128], P('mp'), may hold values from -6 to 6
- cell_surface_share: float32 [8192], P('mp'), may hold values from 0.25 to 4
- band_offsets: int32 [16, 3], replicated, may hold values from -2 to 2, as said below
- latitude_order: int32 [16, 512], P('mp'), may hold values from 0 to 511, each once within a row
Outputs:
- predictions: float32 [8, 8192, 128], P('member', 'mp')
- feature_derivative: float32 [8, 8192, 1024], P('member', 'mp')
- grad_input_weight: float32 [1024, 3072], P(('member', 'mp'))
- grad_output_weight: float32 [1024, 1024], P(('member', 'mp'))
- grad_decoder_weight: float32 [1024, 128], P(('member', 'mp'))
Inputs may be any that keep to these rules, and one draw needn't show every extreme that they name: For each query block b, band_offsets[b] holds 3 different offsets, the first one 0, each with b + offset a block from 0 to 15.
All inputs are finite; a program needn't handle non-finite values.
Results may differ from a plain program's by a relative error of at most 0.024.
Values may be sent and summed in bfloat16 or wider, within the bound.
A program may use at most 128 MiB of HBM per device.

v0:
```python
import functools

import jax
import jax.numpy as jnp
from jax import lax
from jax.experimental import pallas as pl
from jax.experimental.pallas import tpu as pltpu
from jax.sharding import PartitionSpec as P

HEADS = 16
HEAD_DIM = 64
BLOCK = 512
WIDTH = 1024
OUTV = 128
BAND = 3

norm_epsilon = 1e-05
smooth_square = 0.0625

MESH = pl.DeviceIdType.MESH
VMEM_LIMIT = 56 * 1024 * 1024

PIECE = 64
PIECES = BLOCK // PIECE

HALF = 2176
PARTS = ((0, 384), (384, 256), (640, 256), (896, 256), (1152, 256)) + tuple(
    (1408 + 128 * i, 128) for i in range(6)
)
TILE = 16
TILES = 64
CLASSES = 6
ORDER = (1, 3, 2, 4, 0, 5)
FIRST_LINK = (2, 5, 1, 3, 4, 0, 1, 2, 3, 4, 5)
TAIL_VMEM = 60 * 1024 * 1024


def layer_norm(values):
    average = jnp.mean(values, axis=-1, keepdims=True)
    centred = values - average
    spread = jnp.mean(centred * centred, axis=-1, keepdims=True)
    return centred * lax.rsqrt(spread + norm_epsilon)


def softened_derivative(difference):
    return difference * lax.rsqrt(difference * difference + smooth_square)


NT = (((1,), (1,)), ((), ()))


def head_mask(shape, head):
    lane = lax.broadcasted_iota(jnp.int32, shape, 1)
    return (lane // HEAD_DIM) == head


def forward_of_pair(queries, keys, values):
    queries = queries * jnp.bfloat16(0.125)
    values_t = values.T
    sides, tops, totals = [], [], []
    for head in range(2):
        picked = jnp.where(head_mask(queries.shape, head), queries, jnp.bfloat16(0))
        scores = lax.dot_general(keys, picked, NT, preferred_element_type=jnp.float32)
        top = jnp.max(scores, axis=0, keepdims=True)
        powers = jnp.exp(scores - top)
        tops.append(top)
        totals.append(jnp.sum(powers, axis=0, keepdims=True))
        sides.append(
            jnp.dot(
                values_t[head * HEAD_DIM : (head + 1) * HEAD_DIM],
                powers.astype(jnp.bfloat16),
                preferred_element_type=jnp.float32,
            )
        )
    return sides, tops, totals


def place():
    member = lax.axis_index("member")
    mp = lax.axis_index("mp")
    return {
        "z": member // 2,
        "y_hi": member % 2,
        "x": mp // 4,
        "y_lo": (mp // 2) % 2,
        "core": mp % 2,
    }


def device(at):
    return (at["z"] * 2 + at["y_hi"], at["x"] * 4 + at["y_lo"] * 2 + at["core"])


def moved(at, **changes):
    return device({**at, **changes})


def greet(partners):
    barrier = pltpu.get_barrier_semaphore()
    for partner in partners:
        pl.semaphore_signal(barrier, inc=1, device_id=partner, device_id_type=MESH)
    pl.semaphore_wait(barrier, len(partners))


def remote(source, target, send, receive, partner):
    return pltpu.make_async_remote_copy(
        src_ref=source,
        dst_ref=target,
        send_sem=send,
        recv_sem=receive,
        device_id=partner,
        device_id_type=MESH,
    )


def entry_kernel(
    slots,
    raw,
    weights_hbm,
    q_hbm,
    k_own_hbm,
    v_own_hbm,
    k_hbm,
    v_hbm,
    entries_hbm,
    mixed_hbm,
    tops,
    totals,
    q,
    k_own,
    v_own,
    k,
    v,
    entries,
    mixed,
    weights,
    held,
    fetched,
    stored,
    y_send,
    y_recv,
    x_send,
    x_recv,
    c_send,
    c_recv,
    o_send,
    o_recv,
):
    at = place()
    other = moved(at, core=1 - at["core"])
    across = moved(at, y_lo=1 - at["y_lo"])
    forward = moved(at, x=(at["x"] + 1 + 2 * at["y_lo"]) % 4)
    backward = moved(at, x=(at["x"] + 3 - 2 * at["y_lo"]) % 4)
    fetch = pltpu.make_async_copy(weights_hbm, weights, fetched)
    fetch.start()
    greet((other, across, forward, backward))
    near_first = (at["core"] + at["y_lo"]) % 2 == 0
    own = entries.at[pl.ds(0, BLOCK)]

    def store(source, target, place_of):
        return pltpu.make_async_copy(source, target, stored.at[place_of])

    early = [
        store(q, q_hbm, 0),
        store(k_own, k_own_hbm, 1),
        store(v_own, v_own_hbm, 2),
        store(own, entries_hbm.at[pl.ds(0, BLOCK)], 3),
        store(mixed, mixed_hbm, 4),
    ]
    late = [
        [
            store(source.at[pl.ds(begin, BLOCK)], target.at[pl.ds(begin, BLOCK)], 5 + 3 * i + j)
            for j, (source, target, begin) in enumerate(
                (
                    (k, k_hbm, i * BLOCK),
                    (v, v_hbm, i * BLOCK),
                    (entries, entries_hbm, (i + 1) * BLOCK),
                )
            )
        ]
        for i in range(BAND - 1)
    ]

    def rows(piece):
        return pl.ds(pl.multiple_of(piece * PIECE, PIECE), PIECE)

    def to_across(piece):
        return remote(
            own.at[rows(piece)], held.at[1, rows(piece)], y_send.at[piece], y_recv.at[piece], across
        )

    def to_forward(piece):
        return remote(
            held.at[1, rows(piece)],
            held.at[2, rows(piece)],
            x_send.at[piece],
            x_recv.at[piece],
            forward,
        )

    def to_other(slot, piece):
        return remote(
            held.at[slot, rows(piece)],
            held.at[3, rows(piece)],
            c_send.at[piece],
            c_recv.at[piece],
            other,
        )

    def pass_on(piece):
        to_across(piece).wait_recv()
        to_forward(piece).start()

        @pl.when(near_first)
        def _():
            to_other(1, piece).start()

    def project(target, here, source, column):
        def tile(i, carry):
            width = 256
            begin = pl.multiple_of(i * width, width)
            target[here, pl.ds(begin, width)] = jnp.dot(
                source,
                weights[:, pl.ds(pl.multiple_of(column + begin, width), width)],
                preferred_element_type=jnp.float32,
            ).astype(jnp.bfloat16)
            return carry

        lax.fori_loop(0, WIDTH // 256, tile, 0)

    def own_pair(pair, carry):
        here = pl.ds(pl.multiple_of(pair * 2 * HEAD_DIM, 2 * HEAD_DIM), 2 * HEAD_DIM)
        sides, top, total = forward_of_pair(q[:, here], k_own[:, here], v_own[:, here])
        for head in range(2):
            mixed[pair, pl.ds(head * HEAD_DIM, HEAD_DIM)] = sides[head]
            tops[pair, pl.ds(head, 1)] = top[head]
            totals[pair, pl.ds(head, 1)] = total[head]
        pass_on(pair)
        return carry

    def normalise(piece, carry):
        own[rows(piece)] = layer_norm(raw[rows(piece)].astype(jnp.float32)).astype(jnp.bfloat16)
        to_across(piece).start()
        return carry

    lax.fori_loop(0, PIECES, normalise, 0)
    swap = remote(own, held.at[0], o_send, o_recv, other)
    swap.start()
    early[3].start()
    everything = pl.ds(0, BLOCK)
    fetch.wait()
    for i, target in enumerate((q, k_own, v_own)):
        project(target, everything, own[...], i * WIDTH)
        early[i].start()
    lax.fori_loop(0, PIECES, own_pair, 0)
    early[4].start()
    for piece in range(PIECES):
        to_forward(piece).wait_recv()

        @pl.when(jnp.logical_not(near_first))
        def _():
            to_other(2, piece).start()

    for piece in range(PIECES):
        to_other(1, piece).wait_recv()
    swap.wait_recv()
    for i in range(BAND - 1):
        here = pl.ds(i * BLOCK, BLOCK)
        chosen = held[slots[i]]
        entries[pl.ds((i + 1) * BLOCK, BLOCK)] = chosen
        late[i][2].start()
        project(k, here, chosen, WIDTH)
        late[i][0].start()
        project(v, here, chosen, 2 * WIDTH)
        late[i][1].start()
    for copy in early + late[0] + late[1]:
        copy.wait()
    swap.wait_send()
    for piece in range(PIECES):
        to_across(piece).wait_send()
        to_forward(piece).wait_send()
        to_other(1, piece).wait_send()


def entry(slots, own, weights):
    dma = pltpu.SemaphoreType.DMA
    pairs = HEADS // 2

    def half(rows):
        return jax.ShapeDtypeStruct((rows, WIDTH), jnp.bfloat16)

    stat = jax.ShapeDtypeStruct((pairs, 2, BLOCK), jnp.float32)
    return pl.pallas_call(
        entry_kernel,
        out_shape=(
            half(BLOCK),
            half(BLOCK),
            half(BLOCK),
            half(2 * BLOCK),
            half(2 * BLOCK),
            half(3 * BLOCK),
            jax.ShapeDtypeStruct((pairs, 2 * HEAD_DIM, BLOCK), jnp.float32),
            stat,
            stat,
        ),
        in_specs=[
            pl.BlockSpec(memory_space=pltpu.SMEM),
            pl.BlockSpec(memory_space=pltpu.VMEM),
            pl.BlockSpec(memory_space=pl.ANY),
        ],
        out_specs=(pl.BlockSpec(memory_space=pl.ANY),) * 7
        + (pl.BlockSpec(memory_space=pltpu.VMEM),) * 2,
        scratch_shapes=[pltpu.VMEM((count * BLOCK, WIDTH), jnp.bfloat16) for count in (1, 1, 1, 2, 2, 3)]
        + [
            pltpu.VMEM((pairs, 2 * HEAD_DIM, BLOCK), jnp.float32),
            pltpu.VMEM(weights.shape, jnp.bfloat16),
            pltpu.VMEM((4, BLOCK, WIDTH), jnp.bfloat16),
            dma,
            dma((11,)),
        ]
        + [dma((PIECES,))] * 6
        + [dma, dma],
        compiler_params=pltpu.CompilerParams(
            collective_id=0, has_side_effects=True, vmem_limit_bytes=VMEM_LIMIT
        ),
        name="entry",
    )(slots, own, weights)


def crps_kernel(
    predictions,
    target,
    share,
    entries,
    context,
    out,
    entries_t,
    context_t,
    halves,
    gathered,
    grads,
    send,
    receive,
    back_send,
    back_recv,
):
    member = lax.axis_index("member")
    mp = lax.axis_index("mp")
    count = 8
    size = BLOCK // count
    greet([((member + step) % count, mp) for step in range(1, count)])

    def slice_of(index):
        return pl.ds(pl.multiple_of(index * size, size), size)

    def outward(step):
        to = (member + step) % count
        return remote(
            halves.at[slice_of(to)], gathered.at[step], send.at[step], receive.at[step], (to, mp)
        )

    def homeward(step):
        to = (member + count - step) % count
        return remote(
            grads.at[step],
            out.at[slice_of(member)],
            back_send.at[step],
            back_recv.at[step],
            (to, mp),
        )

    halves[...] = predictions[...].astype(jnp.bfloat16)
    for step in range(1, count):
        outward(step).start()
    own = slice_of(member)
    truth = target[own]
    weight = share[own]
    gathered[0] = halves[own]
    for block in range(2):
        here = pl.ds(block * BLOCK, BLOCK)
        entries_t[:, here] = entries[here].T
    for step in range(1, count):
        outward(step).wait_recv()
    each = [gathered[step].astype(jnp.float32) for step in range(count)]
    spread = [0.0] * count
    for one in range(count):
        for two in range(one + 1, count):
            slope = softened_derivative(each[one] - each[two])
            spread[one] = spread[one] + slope
            spread[two] = spread[two] - slope
    for step in range(count):
        single = softened_derivative(each[step] - truth) / count
        paired = spread[step] / (count * (count - 1))
        grads[step] = (weight * (single - paired)).astype(jnp.bfloat16)
        if step:
            homeward(step).start()
    out[own] = grads[0]
    entries_t[:, pl.ds(2 * BLOCK, BLOCK)] = entries[pl.ds(2 * BLOCK, BLOCK)].T
    context_t[...] = context[...].T
    for step in range(1, count):
        homeward(step).wait_recv()
    for step in range(1, count):
        outward(step).wait_send()
        homeward(step).wait_send()


def crps_grad(predictions, target, share, entries, context):
    dma = pltpu.SemaphoreType.DMA
    size = BLOCK // 8
    return pl.pallas_call(
        crps_kernel,
        out_shape=(
            jax.ShapeDtypeStruct(predictions.shape, jnp.bfloat16),
            jax.ShapeDtypeStruct(entries.shape[::-1], jnp.bfloat16),
            jax.ShapeDtypeStruct(context.shape[::-1], jnp.bfloat16),
        ),
        in_specs=[pl.BlockSpec(memory_space=pltpu.VMEM)] * 5,
        out_specs=(pl.BlockSpec(memory_space=pltpu.VMEM),) * 3,
        scratch_shapes=[
            pltpu.VMEM((BLOCK, OUTV), jnp.bfloat16),
            pltpu.VMEM((8, size, OUTV), jnp.bfloat16),
            pltpu.VMEM((8, size, OUTV), jnp.bfloat16),
        ]
        + [dma((8,))] * 4,
        compiler_params=pltpu.CompilerParams(
            collective_id=2, has_side_effects=True, vmem_limit_bytes=VMEM_LIMIT
        ),
        name="crps_grad",
    )(predictions, target, share, entries, context)


def flip(bit, value):
    return (bit + value) % 2


def tail_kernel(
    terms_hbm,
    entries_t_hbm,
    context_t_hbm,
    weights_hbm,
    context_hbm,
    hidden_hbm,
    mid_hbm,
    forecast_hbm,
    q_hbm,
    k_hbm,
    v_hbm,
    grad_context_hbm,
    stats_hbm,
    dq_hbm,
    dk_hbm,
    dv_hbm,
    input_out,
    output_out,
    decoder_out,
    halo_out,
    *scratch,
):
    parts = len(PARTS)
    first_in = scratch[:parts]
    later_in = scratch[parts : 2 * parts]
    total = scratch[2 * parts : 3 * parts]
    other_total = scratch[3 * parts : 4 * parts]
    (
        last,
        last_in,
        grads,
        terms,
        context,
        hidden,
        mid,
        forecast,
        q,
        k,
        v,
        grad_context,
        stats,
        dq,
        dk,
        dv,
        entries_t,
        narrow_t,
        dq_own,
        dk_own,
        dv_own,
        cross_in,
        far_in,
        near_in,
        other_in,
        send,
        receive,
        last_send,
        last_recv,
        y_send,
        y_recv,
        x_send,
        x_recv,
        c_send,
        c_recv,
        o_send,
        o_recv,
        fetched,
    ) = scratch[4 * parts :]
    at = place()
    core = at["core"]
    x_bits = (at["x"] % 2, at["x"] // 2)
    z_bits = (at["z"] % 2, at["z"] // 2)
    y_bits = (at["y_lo"], at["y_hi"])
    other = moved(at, core=1 - core)

    fetches = [
        pltpu.make_async_copy(source, target, fetched.at[i])
        for i, (source, target) in enumerate(
            (
                (terms_hbm, terms),
                (context_t_hbm, narrow_t),
                (hidden_hbm, hidden),
                (mid_hbm, mid),
                (forecast_hbm, forecast),
                (entries_t_hbm, entries_t),
                (context_hbm, context),
                (q_hbm, q),
                (k_hbm, k),
                (v_hbm, v),
                (grad_context_hbm, grad_context),
                (stats_hbm, stats),
                (dq_hbm, dq),
                (dk_hbm, dk),
                (dv_hbm, dv),
            )
        )
    ]
    fetches[0].start()

    def partner_of(link):
        low, high = 1, link // 3
        if link % 3 == 0:
            return moved(at, x=flip(x_bits[0], low) + 2 * flip(x_bits[1], high))
        if link % 3 == 1:
            return moved(at, y_lo=flip(y_bits[0], low), y_hi=flip(y_bits[1], high))
        return moved(at, z=flip(z_bits[0], low) + 2 * flip(z_bits[1], high))

    partners = [partner_of(link) for link in range(CLASSES)]
    greet([other] + partners)

    across = partners[1]
    backward = moved(at, x=(at["x"] + 3 - 2 * at["y_lo"]) % 4)
    near_first = (at["core"] + at["y_lo"]) % 2 == 0

    def rows(piece):
        return pl.ds(piece * PIECE, PIECE)

    def wide(ref, *index):
        return ref[index].astype(jnp.float32)

    def to_other(piece):
        return remote(
            terms.at[3, rows(piece)],
            cross_in.at[rows(piece)],
            c_send.at[piece],
            c_recv.at[piece],
            other,
        )

    def to_backward(piece):
        return remote(
            terms.at[2, rows(piece)], far_in.at[rows(piece)], x_send.at[piece], x_recv.at[piece], backward
        )

    def to_across(piece):
        return remote(
            terms.at[1, rows(piece)], near_in.at[rows(piece)], y_send.at[piece], y_recv.at[piece], across
        )

    swap = remote(terms.at[0], other_in, o_send, o_recv, other)

    def halo_start():
        fetches[0].wait()
        for piece in range(PIECES):
            to_other(piece).start()
        swap.start()
        for fetch in fetches[1:]:
            fetch.start()

    def over_tiles(piece, work):
        def tile(i, carry):
            work(pl.ds(pl.multiple_of(piece * PIECE + i * TILE, TILE), TILE))
            return carry

        lax.fori_loop(0, PIECE // TILE, tile, 0)

    def halo_first(pieces):
        for piece in pieces:
            to_other(piece).wait_recv()

            def add(here):
                cross = wide(cross_in, here)
                terms[2, here] = (wide(terms, 2, here) + jnp.where(near_first, 0.0, cross)).astype(
                    jnp.bfloat16
                )
                terms[1, here] = (wide(terms, 1, here) + jnp.where(near_first, cross, 0.0)).astype(
                    jnp.bfloat16
                )

            over_tiles(piece, add)
            to_backward(piece).start()

    def halo_second(pieces):
        for piece in pieces:
            to_backward(piece).wait_recv()

            def add(here):
                terms[1, here] = (wide(terms, 1, here) + wide(far_in, here)).astype(jnp.bfloat16)

            over_tiles(piece, add)
            to_across(piece).start()

    def halo_end(pieces):
        for piece in pieces:
            to_across(piece).wait_recv()

            def add(here):
                halo_out[here] = halo_out[here] + (wide(other_in, here) + wide(near_in, here))

            over_tiles(piece, add)

    def link_at(part, step):
        return ORDER[(FIRST_LINK[part] + step) % CLASSES]

    weights = (2, 1, 16, 4, 8, 32)
    places = (x_bits[0], y_bits[0], z_bits[0], x_bits[1], y_bits[1], z_bits[1])
    turns = [TILE * weight * (1 - 2 * bit) for weight, bit in zip(weights, places)]
    tile_rows = [TILE * sum(weight * bit for weight, bit in zip(weights, places))]
    for turn in turns:
        tile_rows = tile_rows + [row + turn for row in tile_rows]

    def tile_row(part, position):
        mask = 0
        for step in range(CLASSES):
            if position & (TILES >> (step + 1)):
                link = link_at(part, step)
                mask ^= (1 << link) | (1 << (link % 3))
        return pl.multiple_of(tile_rows[mask], TILE)

    def first_copy(part):
        start, size = PARTS[part]
        return remote(
            grads.at[1 - core, :, pl.ds(start, size)],
            first_in[part],
            send.at[part, 0],
            receive.at[part, 0],
            other,
        )

    def kept(step):
        return (TILES >> step) * TILE

    def pair_of(part, step):
        pair = (total[part], other_total[part])
        return pair if step % 2 else pair[::-1]

    def later_copy(part, step):
        count = kept(step)
        return remote(
            pair_of(part, step)[0].at[pl.ds(count, count)],
            later_in[part].at[pl.ds(count, count)],
            send.at[part, step],
            receive.at[part, step],
            partners[link_at(part, step - 1)],
        )

    def product(terms_of, width, column, half):
        summed = 0.0
        for left, right, begin in terms_of:
            summed = summed + jnp.dot(
                left[...], right[:, pl.ds(begin, width)], preferred_element_type=jnp.float32
            )
        grads[half, :, pl.ds(column, width)] = summed.astype(jnp.bfloat16)

    own_t = entries_t.at[:, pl.ds(0, BLOCK)]
    chosen_t = entries_t.at[:, pl.ds(BLOCK, 2 * BLOCK)]

    def products_of(group):
        column = 640 + 768 * group
        for half in range(2):
            begin = 512 * group + 256 * half
            product([(own_t, dq_own, begin)], 256, column, half)
            product([(own_t, dk_own, begin), (chosen_t, dk, begin)], 256, column + 256, half)
            product([(own_t, dv_own, begin), (chosen_t, dv, begin)], 256, column + 512, half)

    weights = (
        grads.at[0, :, pl.ds(0, WIDTH)],
        grads.at[0, :, pl.ds(WIDTH, WIDTH)],
        grads.at[1, :, pl.ds(0, WIDTH)],
    )
    weight_fetches = [
        pltpu.make_async_copy(
            weights_hbm.at[:, pl.ds(i * WIDTH, WIDTH)], weights[i], fetched.at[len(fetches) + i]
        )
        for i in range(3)
    ]

    def own_part(quarter):
        here = pl.ds(quarter * 256, 256)
        summed = 0.0
        for grad, weight in zip((dq_own, dk_own, dv_own), weights):
            summed = summed + lax.dot_general(
                grad[...], weight[here], NT, preferred_element_type=jnp.float32
            )
        halo_out[:, here] = summed

    def own_pair(pair, carry):
        here = pl.ds(pl.multiple_of(pair * 2 * HEAD_DIM, 2 * HEAD_DIM), 2 * HEAD_DIM)
        queries, grad_keys, grad_values = back_of_pair(
            q[:, here],
            k[:, here],
            v[:, here],
            context[:, here],
            grad_context[:, here],
            [stats[pair, head : head + 1] for head in range(2)],
        )
        dq_own[:, here] = (queries + dq[:, here]).astype(jnp.bfloat16)
        dk_own[:, here] = grad_keys
        dv_own[:, here] = grad_values
        return carry

    def merge_first(part):
        start, size = PARTS[part]
        first_copy(part).wait_recv()

        def merge(positions):
            for position in positions:
                source = pl.ds(tile_row(part, position), TILE)
                total[part][pl.ds(position * TILE, TILE)] = (
                    grads[core, source, pl.ds(start, size)] + first_in[part][source]
                )

        merge(range(TILES // 2, TILES))
        later_copy(part, 1).start()
        merge(range(TILES // 2))

    def merge_later(part, step):
        start, size = PARTS[part]
        count = kept(step)
        held, made = pair_of(part, step)
        later_copy(part, step).wait_recv()
        if step < CLASSES:
            half = count // 2
            for begin in (half, 0):
                made[pl.ds(begin, half)] = (
                    held[pl.ds(begin, half)] + later_in[part][pl.ds(count + begin, half)]
                )
                if begin == half:
                    later_copy(part, step + 1).start()
        else:
            final = wide(held, pl.ds(0, TILE)) + wide(later_in[part], pl.ds(TILE, TILE))
            last[:, :, pl.ds(start, size)] = final.reshape(2, 8, size)

    halo_start()
    fetches[1].wait()
    fetches[2].wait()
    for half in range(2):
        for part in range(2):
            product([(narrow_t, hidden, 512 * half + 256 * part)], 256, 256 * part, half)
    first_copy(0).start()
    halo_first(range(PIECES))
    fetches[3].wait()
    narrow_t[...] = mid[...].T
    fetches[4].wait()
    product([(narrow_t, forecast, 0)], OUTV, 512, 0)
    grads[1, :, pl.ds(512, OUTV)] = jnp.zeros((WIDTH, OUTV), jnp.bfloat16)
    first_copy(1).start()
    fetches[5].wait()
    fetches[6].wait()
    merge_first(0)
    merge_first(1)
    for i in range(7, 13):
        fetches[i].wait()
    lax.fori_loop(0, 4, own_pair, 0)
    halo_second(range(0, 2))
    fetches[13].wait()
    fetches[14].wait()
    products_of(0)
    for part in (2, 3, 4):
        first_copy(part).start()
    merge_later(0, 1)
    merge_later(1, 1)
    halo_second(range(2, 4))
    for part in (2, 3, 4):
        merge_first(part)
    lax.fori_loop(4, 8, own_pair, 0)
    merge_later(0, 2)
    merge_later(1, 2)
    halo_second(range(4, 6))
    for part in (2, 3, 4):
        merge_later(part, 1)
    products_of(1)
    for part in range(5, 11):
        first_copy(part).start()
    merge_later(0, 3)
    merge_later(1, 3)
    for part in (2, 3, 4):
        merge_later(part, 2)
    halo_second(range(6, 8))
    for part in range(5, 11):
        merge_first(part)
    for part in range(parts):
        first_copy(part).wait_send()
    for fetch in weight_fetches:
        fetch.start()
    for step in range(1, CLASSES + 1):
        for part, ahead in ((0, 3), (1, 3), (2, 2), (3, 2), (4, 2)):
            if step + ahead <= CLASSES:
                merge_later(part, step + ahead)
        if step == 1:
            for fetch in weight_fetches:
                fetch.wait()
            for quarter in range(2):
                own_part(quarter)
        if step == 2:
            for quarter in range(2, 4):
                own_part(quarter)
            swap.wait_recv()
        if step >= 3:
            halo_end(range(2 * step - 6, 2 * step - 4))
        for part in range(5, 11):
            merge_later(part, step)
    finish = remote(last.at[1 - core], last_in, last_send, last_recv, other)
    finish.start()

    def deliver(half, source):
        def columns(begin, size):
            return pl.ds(pl.multiple_of(begin, 128), size)

        output_out[:, columns(512 * half, 512)] = source[:, pl.ds(0, 512)]
        for group in range(2):
            for kind in range(3):
                input_out[:, columns(1024 * kind + 512 * group + 256 * half, 256)] = source[
                    :, pl.ds(640 + 768 * group + 256 * kind, 256)
                ]

    deliver(core, last.at[core])
    finish.wait()
    deliver(1 - core, last_in)
    decoder_out[...] = jnp.where(core == 0, last[0, :, pl.ds(512, OUTV)], last_in[:, pl.ds(512, OUTV)])
    swap.wait_send()
    for piece in range(PIECES):
        to_other(piece).wait_send()
        to_backward(piece).wait_send()
        to_across(piece).wait_send()
    for part in range(parts):
        for step in range(1, CLASSES + 1):
            later_copy(part, step).wait_send()


def tail(terms, entries_t, context_t, weights, *others):
    dma = pltpu.SemaphoreType.DMA
    parts = len(PARTS)
    rows = TILES * TILE
    operands = (terms, entries_t, context_t, weights) + others
    blocks = [pltpu.VMEM((rows, size), jnp.bfloat16) for _, size in PARTS]
    block = pltpu.VMEM((BLOCK, WIDTH), jnp.bfloat16)
    return pl.pallas_call(
        tail_kernel,
        out_shape=(
            jax.ShapeDtypeStruct((8, 3 * WIDTH), jnp.float32),
            jax.ShapeDtypeStruct((8, WIDTH), jnp.float32),
            jax.ShapeDtypeStruct((8, OUTV), jnp.float32),
            jax.ShapeDtypeStruct((BLOCK, WIDTH), jnp.float32),
        ),
        in_specs=[pl.BlockSpec(memory_space=pl.ANY)] * len(operands),
        out_specs=(pl.BlockSpec(memory_space=pltpu.VMEM),) * 4,
        scratch_shapes=blocks * 3
        + [pltpu.VMEM((rows // 2, size), jnp.bfloat16) for _, size in PARTS]
        + [
            pltpu.VMEM((2, 8, HALF), jnp.float32),
            pltpu.VMEM((8, HALF), jnp.float32),
            pltpu.VMEM((2, WIDTH, HALF), jnp.bfloat16),
            pltpu.VMEM(terms.shape, terms.dtype),
        ]
        + [pltpu.VMEM(operand.shape, operand.dtype) for operand in others]
        + [
            pltpu.VMEM((WIDTH, BAND * BLOCK), jnp.bfloat16),
            pltpu.VMEM((WIDTH, BLOCK), jnp.bfloat16),
        ]
        + [block] * 7
        + [dma((parts, CLASSES + 1)), dma((parts, CLASSES + 1)), dma, dma]
        + [dma((PIECES,))] * 6
        + [dma, dma, dma((len(operands) + 3,))],
        compiler_params=pltpu.CompilerParams(
            collective_id=1, has_side_effects=True, vmem_limit_bytes=TAIL_VMEM
        ),
        name="tail",
    )(*operands)


def attend_kernel(q_ref, k_ref, v_ref, mixed_ref, top_ref, total_ref, context_ref, stat_ref):
    sides, tops, totals = forward_of_pair(q_ref[...], k_ref[...], v_ref[...])
    whole = []
    for head in range(2):
        own_top = top_ref[0, head : head + 1]
        top = jnp.maximum(own_top, tops[head])
        own_share = jnp.exp(own_top - top)
        share = jnp.exp(tops[head] - top)
        total = own_share * total_ref[0, head : head + 1] + share * totals[head]
        own_mixed = mixed_ref[0, head * HEAD_DIM : (head + 1) * HEAD_DIM]
        whole.append((own_share * own_mixed + share * sides[head]) / total)
        stat_ref[0, head : head + 1] = top + jnp.log(total)
    context_ref[...] = jnp.concatenate(whole, axis=0).T.astype(jnp.bfloat16)


PAIR = 2 * HEAD_DIM


def column_block(rows):
    return pl.BlockSpec((rows, PAIR), lambda i: (0, i))


STAT_BLOCK = pl.BlockSpec((1, 2, BLOCK), lambda i: (i, 0, 0))


def attend(q, k, v, mixed, tops, totals):
    keys = k.shape[0]
    return pl.pallas_call(
        attend_kernel,
        grid=(HEADS // 2,),
        out_shape=(
            jax.ShapeDtypeStruct((BLOCK, WIDTH), jnp.bfloat16),
            jax.ShapeDtypeStruct((HEADS // 2, 2, BLOCK), jnp.float32),
        ),
        in_specs=[column_block(array.shape[0]) for array in (q, k, v)]
        + [pl.BlockSpec((1, PAIR, BLOCK), lambda i: (i, 0, 0)), STAT_BLOCK, STAT_BLOCK],
        out_specs=(column_block(BLOCK), STAT_BLOCK),
        compiler_params=pltpu.CompilerParams(vmem_limit_bytes=VMEM_LIMIT),
        cost_estimate=pl.CostEstimate(
            flops=4 * BLOCK * keys * WIDTH,
            bytes_accessed=2 * WIDTH * (2 * BLOCK + 2 * keys),
            transcendentals=BLOCK * keys * HEADS,
        ),
        name="attend",
    )(q, k, v, mixed, tops, totals)


def back_of_pair(queries, keys, values, context, grads, stats):
    queries = queries * jnp.bfloat16(0.125)
    keys_t = keys.T
    products = (grads.astype(jnp.float32) * context.astype(jnp.float32)).T
    sides = []
    grad_keys = jnp.zeros(keys.shape, jnp.float32)
    grad_values = jnp.zeros(keys.shape, jnp.float32)
    for head in range(2):
        mask = head_mask(queries.shape, head)
        picked = jnp.where(mask, queries, jnp.bfloat16(0))
        grad_here = jnp.where(mask, grads, jnp.bfloat16(0))
        inner = jnp.sum(products[head * HEAD_DIM : (head + 1) * HEAD_DIM], axis=0, keepdims=True)
        scores = lax.dot_general(keys, picked, NT, preferred_element_type=jnp.float32)
        probs = jnp.exp(scores - stats[head])
        grad_probs = lax.dot_general(values, grad_here, NT, preferred_element_type=jnp.float32)
        grad_scores = (probs * (grad_probs - inner)).astype(jnp.bfloat16)
        grad_values += jnp.dot(
            probs.astype(jnp.bfloat16), grad_here, preferred_element_type=jnp.float32
        )
        grad_keys += jnp.dot(grad_scores, picked, preferred_element_type=jnp.float32)
        sides.append(
            jnp.dot(
                keys_t[head * HEAD_DIM : (head + 1) * HEAD_DIM],
                grad_scores,
                preferred_element_type=jnp.float32,
            )
        )
    grad_queries = (jnp.concatenate(sides, axis=0) * 0.125).T
    return grad_queries, grad_keys.astype(jnp.bfloat16), grad_values.astype(jnp.bfloat16)


def attend_back_kernel(q_ref, k_ref, v_ref, context_ref, grad_ref, stat_ref, dq_ref, dk_ref, dv_ref):
    dq_ref[...], dk_ref[...], dv_ref[...] = back_of_pair(
        q_ref[...],
        k_ref[...],
        v_ref[...],
        context_ref[...],
        grad_ref[...],
        [stat_ref[0, head : head + 1] for head in range(2)],
    )


def attend_back(q, k, v, context, grad_context, stats):
    rows, keys = q.shape[0], k.shape[0]
    return pl.pallas_call(
        attend_back_kernel,
        grid=(HEADS // 2,),
        out_shape=(
            jax.ShapeDtypeStruct((rows, WIDTH), jnp.float32),
            jax.ShapeDtypeStruct((keys, WIDTH), jnp.bfloat16),
            jax.ShapeDtypeStruct((keys, WIDTH), jnp.bfloat16),
        ),
        in_specs=[column_block(array.shape[0]) for array in (q, k, v, context, grad_context)]
        + [STAT_BLOCK],
        out_specs=(column_block(rows), column_block(keys), column_block(keys)),
        compiler_params=pltpu.CompilerParams(vmem_limit_bytes=VMEM_LIMIT),
        cost_estimate=pl.CostEstimate(
            flops=10 * rows * keys * WIDTH,
            bytes_accessed=2 * WIDTH * (4 * rows + 4 * keys),
            transcendentals=rows * keys * HEADS,
        ),
        name="attend_back",
    )(q, k, v, context, grad_context, stats)


def chosen_kernel(slots, dk, dv, weights_k, weights_v, terms):
    found = []
    for block in range(2):
        here = pl.ds(block * BLOCK, BLOCK)
        found.append(
            (
                lax.dot_general(dk[here], weights_k[...], NT, preferred_element_type=jnp.float32)
                + lax.dot_general(dv[here], weights_v[...], NT, preferred_element_type=jnp.float32)
            ).astype(jnp.bfloat16)
        )
    for slot in range(4):
        terms[slot] = jnp.zeros(terms.shape[1:], jnp.bfloat16)
    for block in range(2):
        terms[slots[block]] = found[block]


def chosen_terms(slots, dk, dv, weights):
    rows, columns = dk.shape[0], 256
    whole = pl.BlockSpec((rows, WIDTH), lambda i: (0, 0))
    return pl.pallas_call(
        chosen_kernel,
        grid=(WIDTH // columns,),
        out_shape=jax.ShapeDtypeStruct((4, BLOCK, WIDTH), jnp.bfloat16),
        in_specs=[
            pl.BlockSpec(memory_space=pltpu.SMEM),
            whole,
            whole,
            pl.BlockSpec((columns, WIDTH), lambda i: (i, 1)),
            pl.BlockSpec((columns, WIDTH), lambda i: (i, 2)),
        ],
        out_specs=pl.BlockSpec((4, BLOCK, columns), lambda i: (0, 0, i)),
        compiler_params=pltpu.CompilerParams(vmem_limit_bytes=VMEM_LIMIT),
        name="chosen_terms",
    )(slots, dk, dv, weights, weights)


def dot(left, right):
    return jnp.dot(left, right, preferred_element_type=jnp.float32)


def per_device(
    grid_point_features,
    projection_weights_qkv,
    merging_projection,
    readout_weights_table,
    observed,
    cell_surface_share,
    band_offsets,
    latitude_order,
):
    own_rows = grid_point_features[0]
    at = place()
    block = lax.axis_index("mp")
    near, far = jnp.int32(1), jnp.int32(2)
    above = jnp.where(at["y_lo"] == 0, near, far)
    below = jnp.where(at["y_lo"] == 0, far, near)
    minus = jnp.where(at["core"] == 0, 3, 0)
    plus = jnp.where(at["core"] == 0, 0, 3)
    offsets = lax.dynamic_slice(band_offsets, (block, 1), (1, 2))[0]
    slots = jnp.where(
        offsets == -2, below, jnp.where(offsets == -1, minus, jnp.where(offsets == 1, plus, above))
    ).astype(jnp.int32)

    q, k_own, v_own, k, v, entries, mixed, tops, totals = entry(
        slots, own_rows, projection_weights_qkv
    )
    context, stats = attend(q, k, v, mixed, tops, totals)

    hidden = (own_rows.astype(jnp.float32) + dot(context, merging_projection)).astype(jnp.bfloat16)
    normed_mid = layer_norm(hidden.astype(jnp.float32)).astype(jnp.bfloat16)
    predictions = dot(normed_mid, readout_weights_table)
    target = observed[latitude_order[0]]
    grad_forecast, entries_t, context_t = crps_grad(
        predictions, target, cell_surface_share[:, None], entries, context
    )

    grad_mid = dot(grad_forecast, readout_weights_table.T)
    grad_hidden = jax.vjp(layer_norm, hidden.astype(jnp.float32))[1](grad_mid)[0]
    hidden_half = grad_hidden.astype(jnp.bfloat16)
    grad_context = dot(hidden_half, merging_projection.T).astype(jnp.bfloat16)
    dq, dk, dv = attend_back(q, k, v, context, grad_context, stats)

    terms = chosen_terms(slots, dk, dv, projection_weights_qkv)
    grad_input, grad_output, grad_decoder, grad_normed = tail(
        terms,
        entries_t,
        context_t,
        projection_weights_qkv,
        context,
        hidden_half,
        normed_mid,
        grad_forecast,
        q,
        k_own,
        v_own,
        grad_context,
        stats,
        dq,
        dk,
        dv,
    )
    feature_derivative = (
        grad_hidden + jax.vjp(layer_norm, own_rows.astype(jnp.float32))[1](grad_normed)[0]
    )

    return (
        predictions[None],
        feature_derivative[None],
        grad_input,
        grad_output,
        grad_decoder,
    )


def solution(mesh):
    placed = (P("member", "mp", None), P(), P(), P(), P("mp", None), P("mp"), P(), P("mp", None))
    return jax.shard_map(
        per_device,
        mesh=mesh,
        in_specs=placed,
        out_specs=(
            P("member", "mp", None),
            P("member", "mp", None),
            P(("member", "mp"), None),
            P(("member", "mp"), None),
            P(("member", "mp"), None),
        ),
        check_vma=False,
    )
```

profile of v0, /device:TPU:1, one launch (start us, length us, event | category | flops | bytes accessed | tf_op | source)
XLA Modules:
  0.0 222.0 jit_solution(1326250651946096186)
XLA Ops:
  0.6 0.0 copy-start
  0.6 0.0 copy-start.12
  0.7 0.0 copy-start.5
  0.7 1.6 fusion.15.slots
  2.3 0.7 compare_select_fusion
  3.0 1.4 convert_reduce_fusion
  4.4 0.0 copy-done.5
  4.4 1.6 gather_fusion
  6.1 0.0 copy-done.12
  6.1 0.9 copy.13.share
  6.9 46.5 %entry.1 = (bf16[512,1024]{1,0:T(8,128)(2,1)}, bf16[512,1024]{1,0:T(8,128)(2,1)}, bf16[512,1024]{1,0:T(8,128)(2,1)}, bf16[1024,1024]{1,0:T(8,128)(2,1)}, bf16[10...) custom-call(s32[2]{0:T(128)} %fusion.15.slots, ...), custom_call_target="tpu_custom_call" | custom-call | tf_op jit(solution)/shard_map/entry/pallas_call | solution.py:293
  53.4 0.0 copy-start.1
  53.4 18.4 %attend.1 = (bf16[512,1024]{1,0:T(8,128)(2,1)}, f32[8,2,512]{2,1,0:T(2,128)}) custom-call(bf16[512,1024]{1,0:T(8,128)(2,1)} %get-tuple-element.26.q_ref.q_hbm, bf16[1024,1024]{1,0:T(8,128)(2,1)} %get-tuple-element.27.k_ref, bf16[1024,1024]{1,0:T(8,128)(2,1)} %get-tuple-element.28.v_ref, f32[8,128,512]{2,1,0:T(8,128)} %get-tuple-element.29.mixed_ref, ...), custom_call_target="tpu_custom_call" | custom-call | flops 2147483648 | bytes 6291456 | tf_op jit(solution)/shard_map/attend/pallas_call | solution.py:924
  71.8 0.0 copy-done
  71.8 0.0 copy-done.1
  71.8 2.6 %convert_reduce_fusion.1 = (f32[512]{0:T(512)S(1)}, bf16[512,1024]{1,0:T(8,128)(2,1)S(1)}) fusion(bf16[512,1024]{1,0:T(8,128)(2,1)} %get-tuple-element.32.context.context_ref.context_hbm, bf16[1024,1024]{1,0:T(8,128)(2,1)S(1)} %copy-done, bf16[1,512,1024]{2,1,0:T(8,128)(2,1)S(1)} %copy-done.1), kind=kOutput, calls=%fused_computation.10 | convolution fusion | flops 1076362752 | bytes 5244928 | tf_op jit(solution)/shard_map/dot_general | solution.py:1046
  74.4 0.0 copy-start.8
  74.4 0.4 fusion.7
  74.8 0.3 fusion.8.mid_hbm
  75.2 0.2 copy-done.8
  75.4 0.0 copy-start.6
  75.4 1.1 fusion.18.predictions
  76.5 19.8 %crps_grad.1 = (bf16[512,128]{1,0:T(8,128)(2,1)}, bf16[1024,1536]{1,0:T(8,128)(2,1)}, bf16[1024,512]{1,0:T(8,128)(2,1)}) custom-call(f32[512,128]{1,0:T(8,128)} %fusion.18.predictions, f32[512,128]{1,0:T(8,128)} %gather_fusion, f32[512,1]{1,0:T(8,128)} %copy.13.share, bf16[1536,1024]{1,0:T(8,128)(2,1)} %get-tuple-element.33.entries, ...), custom_call_target="tpu_custom_call" | custom-call | tf_op jit(solution)/shard_map/crps_grad/pallas_call | solution.py:410
  96.3 0.0 copy-done.6
  96.3 1.4 fusion.9
  97.7 0.7 fusion.17
  98.4 0.0 copy-start.2
  98.4 1.3 copy-done.2
  99.7 0.2 add_convert_fusion.hidden_hbm
  99.9 0.0 copy-start.7
  99.9 1.0 copy-done.7
  100.9 2.3 %convolution_convert_fusion.grad_ref.grad_context_hbm = bf16[512,1024]{1,0:T(8,128)(2,1)} fusion(bf16[512,1024]{1,0:T(8,128)(2,1)S(1)} %add_convert_fusion.hidden_hbm, bf16[1024,1024]{1,0:T(8,128)(2,1)S(1)} %copy-done), kind=kOutput, calls=%fused_computation.23 | convolution fusion | flops 1074266112 | bytes 4194304 | tf_op jit(solution)/shard_map/dot_general | solution.py:1046
  103.1 24.8 %attend_back.1 = (f32[512,1024]{1,0:T(8,128)}, bf16[1024,1024]{1,0:T(8,128)(2,1)}, bf16[1024,1024]{1,0:T(8,128)(2,1)}) custom-call(bf16[512,1024]{1,0:T(8,128)(2,1)} %get-tuple-element.26.q_ref.q_hbm, bf16[1024,1024]{1,0:T(8,128)(2,1)} %get-tuple-element.27.k_ref, bf16[1024,1024]{1,0:T(8,128)(2,1)} %get-tuple-element.28.v_ref, ...), custom_call_target="tpu_custom_call" | custom-call | flops 5368709120 | bytes 12582912 | tf_op jit(solution)/shard_map/attend_back/pallas_call | solution.py:988
  127.9 9.2 %chosen_terms.1.terms_hbm = bf16[4,512,1024]{2,1,0:T(8,128)(2,1)} custom-call(s32[2]{0:T(128)} %fusion.15.slots, bf16[1024,1024]{1,0:T(8,128)(2,1)} %get-tuple-element.36.dk.dk_hbm, bf16[1024,1024]{1,0:T(8,128)(2,1)} %get-tuple-element.37.dv.dv_hbm, bf16[1024,3072]{1,0:T(8,128)(2,1)} %weights_hbm.3, bf16[1024,3072]{1,0:T(8,128)(2,1)} %weights_hbm.3), custom_call_target="tpu_custom_call" | custom-call | tf_op jit(solution)/shard_map/chosen_terms/pallas_call | solution.py:1028
  137.1 77.0 %tail.1 = (f32[8,3072]{1,0:T(8,128)}, f32[8,1024]{1,0:T(8,128)}, f32[8,128]{1,0:T(8,128)}, f32[512,1024]{1,0:T(8,128)}) custom-call(bf16[4,512,1024]{2,1,0:T(8,128)(2,1)} %chosen_terms.1.terms_hbm, bf16[1024,1536]{1,0:T(8,128)(2,1)} %get-tuple-element.38.entries_t_hbm, bf16[1024,512]{1,0:T(8,128)(2,1)} %get-tuple-element.39.context_t_hbm, ...), custom_call_target="tpu_custom_call" | custom-call | tf_op jit(solution)/shard_map/tail/pallas_call | solution.py:863
  214.2 0.0 copy-start.4
  214.2 2.3 %fusion.10 = (f32[512]{0:T(512)S(1)}, f32[512]{0:T(512)S(1)}) fusion(f32[512]{0:T(512)S(1)} %get-tuple-element.58, bf16[1,512,1024]{2,1,0:T(8,128)(2,1)S(1)} %copy-done.1, f32[512,1024]{1,0:T(8,128)} %get-tuple-element.43), kind=kLoop, calls=%fused_computation.18 | loop fusion | flops 3144704 | bytes 3151872 | tf_op jit(solution)/shard_map/jvp()/reduce_sum | solution.py:41
  216.5 0.0 copy-start.3
  216.6 0.0 copy-done.4
  216.6 0.6 fusion.16
  217.2 0.9 copy-done.3
  218.1 0.0 copy-start.9
  218.1 0.0 copy-start.10
  218.1 0.0 copy-start.11
  218.1 2.0 add_bitcast_fusion
  220.1 0.0 copy-done.9
  220.2 0.6 copy.17
  220.8 0.0 copy-done.10
  220.8 0.6 copy.18
  221.4 0.0 copy-done.11
  221.4 0.6 copy.19
  (7 shorter events, 0.1 us)
Async XLA Ops:
  0.6 71.2 %copy-start = (bf16[1024,1024]{1,0:T(8,128)(2,1)S(1)}, bf16[1024,1024]{1,0:T(8,128)(2,1)}, u32[]{:S(2)}) copy-start(bf16[1024,1024]{1,0:T(8,128)(2,1)} %param.10) | copy-start | bytes 6291460
  0.6 5.4 %copy-start.12 = (f32[512]{0:T(512)S(1)}, f32[512]{0:T(512)}, u32[]{:S(2)}) copy-start(f32[512]{0:T(512)} %param.13) | copy-start | bytes 6148
  0.7 3.7 %copy-start.5 = (f32[512,128]{1,0:T(8,128)S(1)}, f32[512,128]{1,0:T(8,128)}, u32[]{:S(2)}) copy-start(f32[512,128]{1,0:T(8,128)} %param.12) | copy-start | bytes 786436
  53.4 18.4 %copy-start.1 = (bf16[1,512,1024]{2,1,0:T(8,128)(2,1)S(1)}, bf16[1,512,1024]{2,1,0:T(8,128)(2,1)}, u32[]{:S(2)}) copy-start(bf16[1,512,1024]{2,1,0:T(8,128)(2,1)} %param.8) | copy-start | bytes 3145732
  74.4 1.0 copy-start.8
  75.4 20.9 %copy-start.6 = (bf16[512,1024]{1,0:T(8,128)(2,1)}, bf16[512,1024]{1,0:T(8,128)(2,1)S(1)}, u32[]{:S(2)}) copy-start(bf16[512,1024]{1,0:T(8,128)(2,1)S(1)} %fusion.8.mid_hbm) | copy-start | bytes 3145732
  98.4 1.3 copy-start.2
  99.9 1.0 copy-start.7
  214.2 2.4 %copy-start.4 = (f32[512,1024]{1,0:T(8,128)S(1)}, f32[512,1024]{1,0:T(8,128)}, u32[]{:S(2)}) copy-start(f32[512,1024]{1,0:T(8,128)} %get-tuple-element.43) | copy-start | bytes 6291460
  216.5 1.6 copy-start.3
  218.1 2.0 copy-start.9
  218.1 2.7 %copy-start.10 = (f32[8,1024]{1,0:T(8,128)S(1)}, f32[8,1024]{1,0:T(8,128)}, u32[]{:S(2)}) copy-start(f32[8,1024]{1,0:T(8,128)} %get-tuple-element.67) | copy-start | bytes 98308
  218.1 3.3 %copy-start.11 = (f32[8,128]{1,0:T(8,128)S(1)}, f32[8,128]{1,0:T(8,128)}, u32[]{:S(2)}) copy-start(f32[8,128]{1,0:T(8,128)} %get-tuple-element.68) | copy-start | bytes 12292
where the time goes:
time: 223 us; the launch traced here: 222 us
  Pallas kernels  196 us (88%)
  other arithmetic  10.3 us (5%)
  local copies, waits for them, and re-layouts  7.77 us (3%)
  matrix products  7.41 us (3%)
    pallas_call x1, Pallas kernels, tail(): pl.pallas_call(tail_kernel, out_shape=(jax.ShapeDtypeStruct((8, 3 * WIDTH...  77 us
    pallas_call x1, Pallas kernels, entry(): pl.pallas_call(entry_kernel, out_shape=(half(BLOCK), half(BLOCK), half(BL...  46.5 us
    pallas_call x1, Pallas kernels, attend_back(): pl.pallas_call(attend_back_kernel, grid=(HEADS // 2,), out_shape=(jax.Sha...  24.8 us
    pallas_call x1, Pallas kernels, crps_grad(): pl.pallas_call(crps_kernel, out_shape=(jax.ShapeDtypeStruct(predictions.s...  19.8 us
    pallas_call x1, Pallas kernels, attend(): pl.pallas_call(attend_kernel, grid=(HEADS // 2,), out_shape=(jax.ShapeDty...  18.4 us
    pallas_call x1, Pallas kernels, chosen_terms(): pl.pallas_call(chosen_kernel, grid=(WIDTH // columns,), out_shape=jax.Sha...  9.21 us
    dot_general x4, matrix products, dot(): return jnp.dot(left, right, preferred_element_type=jnp.float32)  7.41 us
    unnamed x29, local copies, waits for them, and re-layouts  5.27 us

commit v1 on v0

--- a/solution.py
+++ b/solution.py
@@ -783,46 +783,38 @@
     products_of(0)
     for part in (2, 3, 4):
         first_copy(part).start()
-    merge_later(0, 1)
-    merge_later(1, 1)
     halo_second(range(2, 4))
+    lax.fori_loop(4, 6, own_pair, 0)
     for part in (2, 3, 4):
         merge_first(part)
-    lax.fori_loop(4, 8, own_pair, 0)
-    merge_later(0, 2)
-    merge_later(1, 2)
+    lax.fori_loop(6, 8, own_pair, 0)
     halo_second(range(4, 6))
-    for part in (2, 3, 4):
-        merge_later(part, 1)
     products_of(1)
     for part in range(5, 11):
         first_copy(part).start()
-    merge_later(0, 3)
-    merge_later(1, 3)
-    for part in (2, 3, 4):
-        merge_later(part, 2)
-    halo_second(range(6, 8))
+    merge_later(0, 1)
+    merge_later(1, 1)
     for part in range(5, 11):
         merge_first(part)
     for part in range(parts):
         first_copy(part).wait_send()
     for fetch in weight_fetches:
         fetch.start()
+    halo_second(range(6, 8))
+    for part in (2, 3, 4):
+        merge_later(part, 1)
+    for fetch in weight_fetches:
+        fetch.wait()
     for step in range(1, CLASSES + 1):
-        for part, ahead in ((0, 3), (1, 3), (2, 2), (3, 2), (4, 2)):
+        for part, ahead in ((0, 1), (1, 1), (2, 1), (3, 1), (4, 1)):
             if step + ahead <= CLASSES:
                 merge_later(part, step + ahead)
-        if step == 1:
-            for fetch in weight_fetches:
-                fetch.wait()
-            for quarter in range(2):
-                own_part(quarter)
-        if step == 2:
-            for quarter in range(2, 4):
-                own_part(quarter)
+        if step <= 4:
+            own_part(step - 1)
+        if step == 4:
             swap.wait_recv()
-        if step >= 3:
-            halo_end(range(2 * step - 6, 2 * step - 4))
+        if step >= 5:
+            halo_end(range(4 * step - 20, 4 * step - 16))
         for part in range(5, 11):
             merge_later(part, step)
     finish = remote(last.at[1 - core], last_in, last_send, last_recv, other)

time: 223 us -> 216 us (0.969)
  Pallas kernels: 196 us -> 189 us
    pallas_call x1, Pallas kernels: 77 us -> 70.8 us  [tail(): pl.pallas_call(tail_kernel, out_shape=(jax.ShapeDtypeStruct((8, 3 * WIDTH...]
where the time goes in v1:
time: 216 us
  Pallas kernels  189 us (88%)
  other arithmetic  10.3 us (5%)
  local copies, waits for them, and re-layouts  7.77 us (4%)
  matrix products  7.41 us (3%)
    pallas_call x1, Pallas kernels, tail(): pl.pallas_call(tail_kernel, out_shape=(jax.ShapeDtypeStruct((8, 3 * WIDTH...  70.8 us
    pallas_call x1, Pallas kernels, entry(): pl.pallas_call(entry_kernel, out_shape=(half(BLOCK), half(BLOCK), half(BL...  46.5 us
    pallas_call x1, Pallas kernels, attend_back(): pl.pallas_call(attend_back_kernel, grid=(HEADS // 2,), out_shape=(jax.Sha...  24.8 us
    pallas_call x1, Pallas kernels, crps_grad(): pl.pallas_call(crps_kernel, out_shape=(jax.ShapeDtypeStruct(predictions.s...  19.8 us
    pallas_call x1, Pallas kernels, attend(): pl.pallas_call(attend_kernel, grid=(HEADS // 2,), out_shape=(jax.ShapeDty...  18.4 us
    pallas_call x1, Pallas kernels, chosen_terms(): pl.pallas_call(chosen_kernel, grid=(WIDTH // columns,), out_shape=jax.Sha...  9.21 us
    dot_general x4, matrix products, dot(): return jnp.dot(left, right, preferred_element_type=jnp.float32)  7.41 us
    unnamed x29, local copies, waits for them, and re-layouts  5.27 us

profile of v1, /device:TPU:1, one launch (start us, length us, event | category | flops | bytes accessed | tf_op | source)
XLA Modules:
  0.0 215.8 jit_solution(13302477755894782861)
XLA Ops:
  0.6 0.0 copy-start
  0.6 0.0 copy-start.12
  0.7 0.0 copy-start.5
  0.7 1.6 fusion.15.slots
  2.3 0.7 compare_select_fusion
  3.0 1.4 convert_reduce_fusion
  4.4 0.0 copy-done.5
  4.4 1.6 gather_fusion
  6.1 0.0 copy-done.12
  6.1 0.9 copy.13.share
  6.9 46.5 %entry.1 = (bf16[512,1024]{1,0:T(8,128)(2,1)}, bf16[512,1024]{1,0:T(8,128)(2,1)}, bf16[512,1024]{1,0:T(8,128)(2,1)}, bf16[1024,1024]{1,0:T(8,128)(2,1)}, bf16[10...) custom-call(s32[2]{0:T(128)} %fusion.15.slots, ...), custom_call_target="tpu_custom_call" | custom-call | tf_op jit(solution)/shard_map/entry/pallas_call | solution.py:293
  53.4 0.0 copy-start.1
  53.4 18.4 %attend.1 = (bf16[512,1024]{1,0:T(8,128)(2,1)}, f32[8,2,512]{2,1,0:T(2,128)}) custom-call(bf16[512,1024]{1,0:T(8,128)(2,1)} %get-tuple-element.26.q_ref.q_hbm, bf16[1024,1024]{1,0:T(8,128)(2,1)} %get-tuple-element.27.k_ref, bf16[1024,1024]{1,0:T(8,128)(2,1)} %get-tuple-element.28.v_ref, f32[8,128,512]{2,1,0:T(8,128)} %get-tuple-element.29.mixed_ref, ...), custom_call_target="tpu_custom_call" | custom-call | flops 2147483648 | bytes 6291456 | tf_op jit(solution)/shard_map/attend/pallas_call | solution.py:916
  71.8 0.0 copy-done
  71.8 0.0 copy-done.1
  71.8 2.6 %convert_reduce_fusion.1 = (f32[512]{0:T(512)S(1)}, bf16[512,1024]{1,0:T(8,128)(2,1)S(1)}) fusion(bf16[512,1024]{1,0:T(8,128)(2,1)} %get-tuple-element.32.context.context_ref.context_hbm, bf16[1024,1024]{1,0:T(8,128)(2,1)S(1)} %copy-done, bf16[1,512,1024]{2,1,0:T(8,128)(2,1)S(1)} %copy-done.1), kind=kOutput, calls=%fused_computation.10 | convolution fusion | flops 1076362752 | bytes 5244928 | tf_op jit(solution)/shard_map/dot_general | solution.py:1038
  74.4 0.0 copy-start.8
  74.4 0.4 fusion.7
  74.8 0.3 fusion.8.mid_hbm
  75.2 0.2 copy-done.8
  75.4 0.0 copy-start.6
  75.4 1.1 fusion.18.predictions
  76.5 19.8 %crps_grad.1 = (bf16[512,128]{1,0:T(8,128)(2,1)}, bf16[1024,1536]{1,0:T(8,128)(2,1)}, bf16[1024,512]{1,0:T(8,128)(2,1)}) custom-call(f32[512,128]{1,0:T(8,128)} %fusion.18.predictions, f32[512,128]{1,0:T(8,128)} %gather_fusion, f32[512,1]{1,0:T(8,128)} %copy.13.share, bf16[1536,1024]{1,0:T(8,128)(2,1)} %get-tuple-element.33.entries, ...), custom_call_target="tpu_custom_call" | custom-call | tf_op jit(solution)/shard_map/crps_grad/pallas_call | solution.py:410
  96.3 0.0 copy-done.6
  96.3 1.4 fusion.9
  97.7 0.7 fusion.17
  98.4 0.0 copy-start.2
  98.4 1.3 copy-done.2
  99.7 0.2 add_convert_fusion.hidden_hbm
  99.9 0.0 copy-start.7
  99.9 1.0 copy-done.7
  100.9 2.3 %convolution_convert_fusion.grad_ref.grad_context_hbm = bf16[512,1024]{1,0:T(8,128)(2,1)} fusion(bf16[512,1024]{1,0:T(8,128)(2,1)S(1)} %add_convert_fusion.hidden_hbm, bf16[1024,1024]{1,0:T(8,128)(2,1)S(1)} %copy-done), kind=kOutput, calls=%fused_computation.23 | convolution fusion | flops 1074266112 | bytes 4194304 | tf_op jit(solution)/shard_map/dot_general | solution.py:1038
  103.1 24.8 %attend_back.1 = (f32[512,1024]{1,0:T(8,128)}, bf16[1024,1024]{1,0:T(8,128)(2,1)}, bf16[1024,1024]{1,0:T(8,128)(2,1)}) custom-call(bf16[512,1024]{1,0:T(8,128)(2,1)} %get-tuple-element.26.q_ref.q_hbm, bf16[1024,1024]{1,0:T(8,128)(2,1)} %get-tuple-element.27.k_ref, bf16[1024,1024]{1,0:T(8,128)(2,1)} %get-tuple-element.28.v_ref, ...), custom_call_target="tpu_custom_call" | custom-call | flops 5368709120 | bytes 12582912 | tf_op jit(solution)/shard_map/attend_back/pallas_call | solution.py:980
  127.9 9.2 %chosen_terms.1.terms_hbm = bf16[4,512,1024]{2,1,0:T(8,128)(2,1)} custom-call(s32[2]{0:T(128)} %fusion.15.slots, bf16[1024,1024]{1,0:T(8,128)(2,1)} %get-tuple-element.36.dk.dk_hbm, bf16[1024,1024]{1,0:T(8,128)(2,1)} %get-tuple-element.37.dv.dv_hbm, bf16[1024,3072]{1,0:T(8,128)(2,1)} %weights_hbm.3, bf16[1024,3072]{1,0:T(8,128)(2,1)} %weights_hbm.3), custom_call_target="tpu_custom_call" | custom-call | tf_op jit(solution)/shard_map/chosen_terms/pallas_call | solution.py:1020
  137.1 70.8 %tail.1 = (f32[8,3072]{1,0:T(8,128)}, f32[8,1024]{1,0:T(8,128)}, f32[8,128]{1,0:T(8,128)}, f32[512,1024]{1,0:T(8,128)}) custom-call(bf16[4,512,1024]{2,1,0:T(8,128)(2,1)} %chosen_terms.1.terms_hbm, bf16[1024,1536]{1,0:T(8,128)(2,1)} %get-tuple-element.38.entries_t_hbm, bf16[1024,512]{1,0:T(8,128)(2,1)} %get-tuple-element.39.context_t_hbm, ...), custom_call_target="tpu_custom_call" | custom-call | tf_op jit(solution)/shard_map/tail/pallas_call | solution.py:855
  207.9 0.0 copy-start.4
  207.9 2.3 %fusion.10 = (f32[512]{0:T(512)S(1)}, f32[512]{0:T(512)S(1)}) fusion(f32[512]{0:T(512)S(1)} %get-tuple-element.58, bf16[1,512,1024]{2,1,0:T(8,128)(2,1)S(1)} %copy-done.1, f32[512,1024]{1,0:T(8,128)} %get-tuple-element.43), kind=kLoop, calls=%fused_computation.18 | loop fusion | flops 3144704 | bytes 3151872 | tf_op jit(solution)/shard_map/jvp()/reduce_sum | solution.py:41
  210.3 0.0 copy-start.3
  210.3 0.0 copy-done.4
  210.3 0.6 fusion.16
  211.0 0.9 copy-done.3
  211.9 0.0 copy-start.9
  211.9 0.0 copy-start.10
  211.9 0.0 copy-start.11
  211.9 2.0 add_bitcast_fusion
  213.9 0.0 copy-done.9
  213.9 0.6 copy.17
  214.5 0.0 copy-done.10
  214.6 0.6 copy.18
  215.2 0.0 copy-done.11
  215.2 0.6 copy.19
  (7 shorter events, 0.1 us)
Async XLA Ops:
  0.6 71.2 %copy-start = (bf16[1024,1024]{1,0:T(8,128)(2,1)S(1)}, bf16[1024,1024]{1,0:T(8,128)(2,1)}, u32[]{:S(2)}) copy-start(bf16[1024,1024]{1,0:T(8,128)(2,1)} %param.10) | copy-start | bytes 6291460
  0.6 5.4 %copy-start.12 = (f32[512]{0:T(512)S(1)}, f32[512]{0:T(512)}, u32[]{:S(2)}) copy-start(f32[512]{0:T(512)} %param.13) | copy-start | bytes 6148
  0.7 3.7 %copy-start.5 = (f32[512,128]{1,0:T(8,128)S(1)}, f32[512,128]{1,0:T(8,128)}, u32[]{:S(2)}) copy-start(f32[512,128]{1,0:T(8,128)} %param.12) | copy-start | bytes 786436
  53.4 18.4 %copy-start.1 = (bf16[1,512,1024]{2,1,0:T(8,128)(2,1)S(1)}, bf16[1,512,1024]{2,1,0:T(8,128)(2,1)}, u32[]{:S(2)}) copy-start(bf16[1,512,1024]{2,1,0:T(8,128)(2,1)} %param.8) | copy-start | bytes 3145732
  74.4 1.0 copy-start.8
  75.4 20.9 %copy-start.6 = (bf16[512,1024]{1,0:T(8,128)(2,1)}, bf16[512,1024]{1,0:T(8,128)(2,1)S(1)}, u32[]{:S(2)}) copy-start(bf16[512,1024]{1,0:T(8,128)(2,1)S(1)} %fusion.8.mid_hbm) | copy-start | bytes 3145732
  98.4 1.3 copy-start.2
  99.9 1.0 copy-start.7
  207.9 2.4 %copy-start.4 = (f32[512,1024]{1,0:T(8,128)S(1)}, f32[512,1024]{1,0:T(8,128)}, u32[]{:S(2)}) copy-start(f32[512,1024]{1,0:T(8,128)} %get-tuple-element.43) | copy-start | bytes 6291460
  210.3 1.6 copy-start.3
  211.9 2.0 copy-start.9
  211.9 2.7 %copy-start.10 = (f32[8,1024]{1,0:T(8,128)S(1)}, f32[8,1024]{1,0:T(8,128)}, u32[]{:S(2)}) copy-start(f32[8,1024]{1,0:T(8,128)} %get-tuple-element.67) | copy-start | bytes 98308
  211.9 3.3 %copy-start.11 = (f32[8,128]{1,0:T(8,128)S(1)}, f32[8,128]{1,0:T(8,128)}, u32[]{:S(2)}) copy-start(f32[8,128]{1,0:T(8,128)} %get-tuple-element.68) | copy-start | bytes 12292

commit v2 on v1

--- a/solution.py
+++ b/solution.py
@@ -265,14 +265,13 @@
         to_other(1, piece).wait_recv()
     swap.wait_recv()
     for i in range(BAND - 1):
-        here = pl.ds(i * BLOCK, BLOCK)
-        chosen = held[slots[i]]
-        entries[pl.ds((i + 1) * BLOCK, BLOCK)] = chosen
+        entries[pl.ds((i + 1) * BLOCK, BLOCK)] = held[slots[i]]
         late[i][2].start()
-        project(k, here, chosen, WIDTH)
-        late[i][0].start()
-        project(v, here, chosen, 2 * WIDTH)
-        late[i][1].start()
+    chosen = entries[pl.ds(BLOCK, 2 * BLOCK)]
+    for j, target in enumerate((k, v)):
+        project(target, pl.ds(0, 2 * BLOCK), chosen, (j + 1) * WIDTH)
+        late[0][j].start()
+        late[1][j].start()
     for copy in early + late[0] + late[1]:
         copy.wait()
     swap.wait_send()

time: 216 us -> 215 us (level)
  no operation moved by 1% of the time
where the time goes in v2:
time: 215 us
  Pallas kernels  188 us (87%)
  other arithmetic  10.3 us (5%)
  local copies, waits for them, and re-layouts  7.77 us (4%)
  matrix products  7.42 us (3%)
    pallas_call x1, Pallas kernels, tail(): pl.pallas_call(tail_kernel, out_shape=(jax.ShapeDtypeStruct((8, 3 * WIDTH...  71 us
    pallas_call x1, Pallas kernels, entry(): pl.pallas_call(entry_kernel, out_shape=(half(BLOCK), half(BLOCK), half(BL...  45.3 us
    pallas_call x1, Pallas kernels, attend_back(): pl.pallas_call(attend_back_kernel, grid=(HEADS // 2,), out_shape=(jax.Sha...  24.8 us
    pallas_call x1, Pallas kernels, crps_grad(): pl.pallas_call(crps_kernel, out_shape=(jax.ShapeDtypeStruct(predictions.s...  19.6 us
    pallas_call x1, Pallas kernels, attend(): pl.pallas_call(attend_kernel, grid=(HEADS // 2,), out_shape=(jax.ShapeDty...  18.4 us
    pallas_call x1, Pallas kernels, chosen_terms(): pl.pallas_call(chosen_kernel, grid=(WIDTH // columns,), out_shape=jax.Sha...  9.21 us
    dot_general x4, matrix products, dot(): return jnp.dot(left, right, preferred_element_type=jnp.float32)  7.42 us
    unnamed x29, local copies, waits for them, and re-layouts  5.27 us

profile of v2, /device:TPU:1, one launch (start us, length us, event | category | flops | bytes accessed | tf_op | source)
XLA Modules:
  0.0 214.6 jit_solution(1635504680293672378)
XLA Ops:
  0.6 0.0 copy-start
  0.6 0.0 copy-start.12
  0.7 0.0 copy-start.5
  0.7 1.6 fusion.15.slots
  2.3 0.7 compare_select_fusion
  3.0 1.4 convert_reduce_fusion
  4.4 0.0 copy-done.5
  4.4 1.6 gather_fusion
  6.1 0.0 copy-done.12
  6.1 0.9 copy.13.share
  6.9 45.3 %entry.1 = (bf16[512,1024]{1,0:T(8,128)(2,1)}, bf16[512,1024]{1,0:T(8,128)(2,1)}, bf16[512,1024]{1,0:T(8,128)(2,1)}, bf16[1024,1024]{1,0:T(8,128)(2,1)}, bf16[10...) custom-call(s32[2]{0:T(128)} %fusion.15.slots, ...), custom_call_target="tpu_custom_call" | custom-call | tf_op jit(solution)/shard_map/entry/pallas_call | solution.py:292
  52.2 0.0 copy-start.1
  52.2 18.4 %attend.1 = (bf16[512,1024]{1,0:T(8,128)(2,1)}, f32[8,2,512]{2,1,0:T(2,128)}) custom-call(bf16[512,1024]{1,0:T(8,128)(2,1)} %get-tuple-element.26.q_ref.q_hbm, bf16[1024,1024]{1,0:T(8,128)(2,1)} %get-tuple-element.27.k_ref, bf16[1024,1024]{1,0:T(8,128)(2,1)} %get-tuple-element.28.v_ref, f32[8,128,512]{2,1,0:T(8,128)} %get-tuple-element.29.mixed_ref, ...), custom_call_target="tpu_custom_call" | custom-call | flops 2147483648 | bytes 6291456 | tf_op jit(solution)/shard_map/attend/pallas_call | solution.py:915
  70.6 0.0 copy-done
  70.6 0.0 copy-done.1
  70.6 2.6 %convert_reduce_fusion.1 = (f32[512]{0:T(512)S(1)}, bf16[512,1024]{1,0:T(8,128)(2,1)S(1)}) fusion(bf16[512,1024]{1,0:T(8,128)(2,1)} %get-tuple-element.32.context.context_ref.context_hbm, bf16[1024,1024]{1,0:T(8,128)(2,1)S(1)} %copy-done, bf16[1,512,1024]{2,1,0:T(8,128)(2,1)S(1)} %copy-done.1), kind=kOutput, calls=%fused_computation.10 | convolution fusion | flops 1076362752 | bytes 5244928 | tf_op jit(solution)/shard_map/dot_general | solution.py:1037
  73.2 0.0 copy-start.8
  73.2 0.4 fusion.7
  73.6 0.3 fusion.8.mid_hbm
  73.9 0.2 copy-done.8
  74.1 0.0 copy-start.6
  74.1 1.1 fusion.18.predictions
  75.3 19.6 %crps_grad.1 = (bf16[512,128]{1,0:T(8,128)(2,1)}, bf16[1024,1536]{1,0:T(8,128)(2,1)}, bf16[1024,512]{1,0:T(8,128)(2,1)}) custom-call(f32[512,128]{1,0:T(8,128)} %fusion.18.predictions, f32[512,128]{1,0:T(8,128)} %gather_fusion, f32[512,1]{1,0:T(8,128)} %copy.13.share, bf16[1536,1024]{1,0:T(8,128)(2,1)} %get-tuple-element.33.entries, ...), custom_call_target="tpu_custom_call" | custom-call | tf_op jit(solution)/shard_map/crps_grad/pallas_call | solution.py:409
  94.9 0.0 copy-done.6
  94.9 1.4 fusion.9
  96.4 0.7 fusion.17
  97.0 0.0 copy-start.2
  97.0 1.3 copy-done.2
  98.3 0.2 add_convert_fusion.hidden_hbm
  98.5 0.0 copy-start.7
  98.5 1.0 copy-done.7
  99.5 2.3 %convolution_convert_fusion.grad_ref.grad_context_hbm = bf16[512,1024]{1,0:T(8,128)(2,1)} fusion(bf16[512,1024]{1,0:T(8,128)(2,1)S(1)} %add_convert_fusion.hidden_hbm, bf16[1024,1024]{1,0:T(8,128)(2,1)S(1)} %copy-done), kind=kOutput, calls=%fused_computation.23 | convolution fusion | flops 1074266112 | bytes 4194304 | tf_op jit(solution)/shard_map/dot_general | solution.py:1037
  101.8 24.8 %attend_back.1 = (f32[512,1024]{1,0:T(8,128)}, bf16[1024,1024]{1,0:T(8,128)(2,1)}, bf16[1024,1024]{1,0:T(8,128)(2,1)}) custom-call(bf16[512,1024]{1,0:T(8,128)(2,1)} %get-tuple-element.26.q_ref.q_hbm, bf16[1024,1024]{1,0:T(8,128)(2,1)} %get-tuple-element.27.k_ref, bf16[1024,1024]{1,0:T(8,128)(2,1)} %get-tuple-element.28.v_ref, ...), custom_call_target="tpu_custom_call" | custom-call | flops 5368709120 | bytes 12582912 | tf_op jit(solution)/shard_map/attend_back/pallas_call | solution.py:979
  126.6 9.2 %chosen_terms.1.terms_hbm = bf16[4,512,1024]{2,1,0:T(8,128)(2,1)} custom-call(s32[2]{0:T(128)} %fusion.15.slots, bf16[1024,1024]{1,0:T(8,128)(2,1)} %get-tuple-element.36.dk.dk_hbm, bf16[1024,1024]{1,0:T(8,128)(2,1)} %get-tuple-element.37.dv.dv_hbm, bf16[1024,3072]{1,0:T(8,128)(2,1)} %weights_hbm.3, bf16[1024,3072]{1,0:T(8,128)(2,1)} %weights_hbm.3), custom_call_target="tpu_custom_call" | custom-call | tf_op jit(solution)/shard_map/chosen_terms/pallas_call | solution.py:1019
  135.8 71.0 %tail.1 = (f32[8,3072]{1,0:T(8,128)}, f32[8,1024]{1,0:T(8,128)}, f32[8,128]{1,0:T(8,128)}, f32[512,1024]{1,0:T(8,128)}) custom-call(bf16[4,512,1024]{2,1,0:T(8,128)(2,1)} %chosen_terms.1.terms_hbm, bf16[1024,1536]{1,0:T(8,128)(2,1)} %get-tuple-element.38.entries_t_hbm, bf16[1024,512]{1,0:T(8,128)(2,1)} %get-tuple-element.39.context_t_hbm, ...), custom_call_target="tpu_custom_call" | custom-call | tf_op jit(solution)/shard_map/tail/pallas_call | solution.py:854
  206.8 0.0 copy-start.4
  206.8 2.3 %fusion.10 = (f32[512]{0:T(512)S(1)}, f32[512]{0:T(512)S(1)}) fusion(f32[512]{0:T(512)S(1)} %get-tuple-element.58, bf16[1,512,1024]{2,1,0:T(8,128)(2,1)S(1)} %copy-done.1, f32[512,1024]{1,0:T(8,128)} %get-tuple-element.43), kind=kLoop, calls=%fused_computation.18 | loop fusion | flops 3144704 | bytes 3151872 | tf_op jit(solution)/shard_map/jvp()/reduce_sum | solution.py:41
  209.1 0.0 copy-start.3
  209.1 0.0 copy-done.4
  209.2 0.6 fusion.16
  209.8 0.9 copy-done.3
  210.7 0.0 copy-start.9
  210.7 0.0 copy-start.10
  210.7 0.0 copy-start.11
  210.7 2.0 add_bitcast_fusion
  212.7 0.0 copy-done.9
  212.7 0.6 copy.17
  213.4 0.0 copy-done.10
  213.4 0.6 copy.18
  214.0 0.0 copy-done.11
  214.0 0.6 copy.19
  (7 shorter events, 0.1 us)
Async XLA Ops:
  0.6 70.0 %copy-start = (bf16[1024,1024]{1,0:T(8,128)(2,1)S(1)}, bf16[1024,1024]{1,0:T(8,128)(2,1)}, u32[]{:S(2)}) copy-start(bf16[1024,1024]{1,0:T(8,128)(2,1)} %param.10) | copy-start | bytes 6291460
  0.6 5.4 %copy-start.12 = (f32[512]{0:T(512)S(1)}, f32[512]{0:T(512)}, u32[]{:S(2)}) copy-start(f32[512]{0:T(512)} %param.13) | copy-start | bytes 6148
  0.7 3.7 %copy-start.5 = (f32[512,128]{1,0:T(8,128)S(1)}, f32[512,128]{1,0:T(8,128)}, u32[]{:S(2)}) copy-start(f32[512,128]{1,0:T(8,128)} %param.12) | copy-start | bytes 786436
  52.2 18.4 %copy-start.1 = (bf16[1,512,1024]{2,1,0:T(8,128)(2,1)S(1)}, bf16[1,512,1024]{2,1,0:T(8,128)(2,1)}, u32[]{:S(2)}) copy-start(bf16[1,512,1024]{2,1,0:T(8,128)(2,1)} %param.8) | copy-start | bytes 3145732
  73.2 1.0 copy-start.8
  74.1 20.8 %copy-start.6 = (bf16[512,1024]{1,0:T(8,128)(2,1)}, bf16[512,1024]{1,0:T(8,128)(2,1)S(1)}, u32[]{:S(2)}) copy-start(bf16[512,1024]{1,0:T(8,128)(2,1)S(1)} %fusion.8.mid_hbm) | copy-start | bytes 3145732
  97.0 1.3 copy-start.2
  98.5 1.0 copy-start.7
  206.8 2.4 %copy-start.4 = (f32[512,1024]{1,0:T(8,128)S(1)}, f32[512,1024]{1,0:T(8,128)}, u32[]{:S(2)}) copy-start(f32[512,1024]{1,0:T(8,128)} %get-tuple-element.43) | copy-start | bytes 6291460
  209.1 1.6 copy-start.3
  210.7 2.0 copy-start.9
  210.7 2.7 %copy-start.10 = (f32[8,1024]{1,0:T(8,128)S(1)}, f32[8,1024]{1,0:T(8,128)}, u32[]{:S(2)}) copy-start(f32[8,1024]{1,0:T(8,128)} %get-tuple-element.67) | copy-start | bytes 98308
  210.7 3.3 %copy-start.11 = (f32[8,128]{1,0:T(8,128)S(1)}, f32[8,128]{1,0:T(8,128)}, u32[]{:S(2)}) copy-start(f32[8,128]{1,0:T(8,128)} %get-tuple-element.68) | copy-start | bytes 12292
